TPU v7x, 32 devices: a whole 2x2x4 slice. The times are simulated.
32 devices in a mesh: ctx: 8 (over z, x), ch: 4 (over y, core).
Axes of the slice: x: 2, y: 2, z: 4, core: 2. Of those that a mesh axis runs over, the one named last changes fastest.
Arguments:
- x_slab: bfloat16 [8192, 1024], P('ch', 'ctx'), may hold values from -6 to 6
- filter_taps: float32 [128, 1024], P('ch', 'ctx'), may hold values from -0.1875 to 0.1875
- mix_weight: bfloat16 [8192, 3, 128], P('ch'), may hold values from -0.0625 to 0.0625
- skip_gain: float32 [128], P('ch'), may hold values from 0.25 to 1.5
- cotangent: bfloat16 [128, 1024], P('ch', 'ctx'), may hold values from -6 to 6
Outputs:
- input_grad: bfloat16 [8192, 1024], P('ch', 'ctx')
- weight_grad: float32 [8192, 3, 128], P(('ch', 'ctx'))
- filter_grad: float32 [128, 1024], P('ch', 'ctx')
All inputs are finite; a program needn't handle non-finite values.
Results may differ from a plain program's by a relative error of at most 0.005.
Values may be sent and summed in bfloat16 or wider, within the bound.
A program may use at most 64 MiB of HBM per device.

v0:
```python
import math

import jax
import jax.numpy as jnp
from jax import lax
from jax.sharding import PartitionSpec as P

highest = lax.Precision.HIGHEST


def angle_table(rows, cols, period):
    product = (
        jnp.arange(rows, dtype=jnp.int32)[:, None]
        * jnp.arange(cols, dtype=jnp.int32)[None, :]
        % period
    )
    phase = product.astype(jnp.float32) * (2.0 * math.pi / period)
    return (jnp.cos(phase), jnp.sin(phase))


def twiddle(count, width):
    span = width // count
    places = lax.axis_index("ctx") * span + jnp.arange(span, dtype=jnp.int32)
    total = 2 * count * width
    product = jnp.arange(2 * count, dtype=jnp.int32)[:, None] * places[None, :] % total
    phase = product.astype(jnp.float32) * (2.0 * math.pi / total)
    return (jnp.cos(phase), jnp.sin(phase))


def spread(fields):
    return lax.all_to_all(fields[:, None, :], "ctx", split_axis=2, concat_axis=1, tiled=True)


def gather_back(parted):
    joined = lax.all_to_all(parted, "ctx", split_axis=1, concat_axis=2, tiled=True)
    return joined[:, 0, :]


def spectrum(parted):
    count = parted.shape[1]
    width = count * parted.shape[2]
    cos_j, sin_j = angle_table(count, 2 * count, 2 * count)
    real_part = jnp.einsum("rjs,jk->rks", parted, cos_j, precision=highest)
    imag_part = -jnp.einsum("rjs,jk->rks", parted, sin_j, precision=highest)
    cos_t, sin_t = twiddle(count, width)
    turned = jnp.stack(
        [real_part * cos_t + imag_part * sin_t, imag_part * cos_t - real_part * sin_t]
    )
    moved = lax.all_to_all(turned, "ctx", split_axis=2, concat_axis=3, tiled=True)
    cos_b, sin_b = angle_table(width, width, width)
    real_out = jnp.einsum("rkb,bm->rkm", moved[0], cos_b, precision=highest) + jnp.einsum(
        "rkb,bm->rkm", moved[1], sin_b, precision=highest
    )
    imag_out = jnp.einsum("rkb,bm->rkm", moved[1], cos_b, precision=highest) - jnp.einsum(
        "rkb,bm->rkm", moved[0], sin_b, precision=highest
    )
    return jnp.stack([real_out, imag_out])


def unspectrum(spec):
    count = lax.axis_size("ctx")
    width = spec.shape[3]
    cos_b, sin_b = angle_table(width, width, width)
    real_part = jnp.einsum("rkm,mb->rkb", spec[0], cos_b, precision=highest) - jnp.einsum(
        "rkm,mb->rkb", spec[1], sin_b, precision=highest
    )
    imag_part = jnp.einsum("rkm,mb->rkb", spec[1], cos_b, precision=highest) + jnp.einsum(
        "rkm,mb->rkb", spec[0], sin_b, precision=highest
    )
    moved = lax.all_to_all(
        jnp.stack([real_part, imag_part]), "ctx", split_axis=3, concat_axis=2, tiled=True
    )
    cos_t, sin_t = twiddle(count, width)
    real_turn = moved[0] * cos_t - moved[1] * sin_t
    imag_turn = moved[1] * cos_t + moved[0] * sin_t
    cos_j, sin_j = angle_table(2 * count, count, 2 * count)
    summed = jnp.einsum("rks,kj->rjs", real_turn, cos_j, precision=highest) - jnp.einsum(
        "rks,kj->rjs", imag_turn, sin_j, precision=highest
    )
    return summed / float(2 * count * width)


def times_spec(left, right):
    return jnp.stack(
        [left[0] * right[0] - left[1] * right[1], left[0] * right[1] + left[1] * right[0]]
    )


def times_conj(left, right):
    return jnp.stack(
        [left[0] * right[0] + left[1] * right[1], left[1] * right[0] - left[0] * right[1]]
    )


def shards(x_slab, filter_taps, mix_weight, skip_gain, cotangent):
    chans = cotangent.shape[0]
    width = cotangent.shape[1]
    count = lax.axis_size("ctx")
    piece = mix_weight
    projected = lax.psum_scatter(
        jnp.einsum("ijo,il->ojl", piece, x_slab, preferred_element_type=jnp.float32),
        "ch",
        scatter_dimension=0,
        tiled=True,
    )
    outer_gate = projected[:, 0]
    inner_gate = projected[:, 1]
    values_in = projected[:, 2]
    product = inner_gate * values_in
    grad_out = cotangent.astype(jnp.float32)
    gain = skip_gain[:, None]
    spectra_all = spectrum(spread(jnp.concatenate([product, filter_taps], 0)))
    prod_spec = spectra_all[:, :chans]
    filt_spec = spectra_all[:, chans:]
    convolved = gather_back(unspectrum(times_spec(prod_spec, filt_spec)))
    mixed = convolved + gain * product
    grad_mixed = grad_out * outer_gate
    grad_outer = grad_out * mixed
    grad_spec = spectrum(spread(grad_mixed))
    adjoint = gather_back(
        unspectrum(
            jnp.concatenate([times_conj(grad_spec, filt_spec), times_conj(grad_spec, prod_spec)], 1)
        )
    )
    grad_product = adjoint[:chans] + gain * grad_mixed
    grad_filter = adjoint[chans:]
    grad_proj = jnp.stack(
        [grad_outer, grad_product * values_in, grad_product * inner_gate], 1
    ).astype(jnp.bfloat16)
    all_grads = lax.all_gather(grad_proj, "ch", axis=0, tiled=True)
    scale = 1.0 / math.sqrt(count * width)
    piece = x_slab
    weight_grad = lax.psum_scatter(
        jnp.einsum("il,ojl->ijo", piece, all_grads, preferred_element_type=jnp.float32) * scale,
        "ctx",
        scatter_dimension=0,
        tiled=True,
    )
    input_grad = jnp.einsum(
        "ijo,ojl->il", mix_weight, all_grads, preferred_element_type=jnp.float32
    )
    return (input_grad.astype(jnp.bfloat16), weight_grad, grad_filter * scale)


def solution(mesh):
    in_specs = (P("ch", "ctx"), P("ch", "ctx"), P("ch", None, None), P("ch"), P("ch", "ctx"))
    out_specs = (P("ch", "ctx"), P(("ch", "ctx"), None, None), P("ch", "ctx"))
    return jax.shard_map(shards, mesh=mesh, in_specs=in_specs, out_specs=out_specs, check_vma=False)
```

profile of v0, /device:TPU:1, one launch (start us, length us, event | category | flops | bytes accessed | tf_op | source)
XLA Modules:
  0.0 228.1 jit_solution(6064494929353579322)
XLA Ops:
  7.3 1.3 copy-done
  8.6 1.5 convolution_bitcast_fusion.1
  12.7 30.9 %all-reduce.3.cloned.1.call-done = f32[128,3,128]{2,1,0:T(4,128)} async-done(((f32[128,3,128]{2,1,0:T(4,128)}), f32[128,3,128]{2,1,0:T(4,128)}) %all-reduce.3.cloned.1.call-update) | async-done | bytes 196624
  47.1 5.6 %all-to-all-start.4 = ((f32[8,1,512]{2,1,0:T(1,128)}), f32[8,1,512]{2,1,0:T(1,128)S(1)}, u32[]{:S(2)}, u32[]{:S(2)}) async-start(f32[8,1,512]{2,1,0:T(1,128)} %reshape.110), calls=%async_computation.4 | async-start | bytes 32768 | tf_op jit(solution)/shard_map/all_to_all | solution.py:31
  54.4 3.8 %all-to-all-done.4 = f32[8,1,512]{2,1,0:T(1,128)S(1)} async-done(((f32[8,1,512]{2,1,0:T(1,128)}), f32[8,1,512]{2,1,0:T(1,128)S(1)}, u32[]{:S(2)}, u32[]{:S(2)}) %all-to-all-start.4) | async-done | bytes 16416 | tf_op jit(solution)/shard_map/all_to_all | solution.py:31
  58.2 3.3 %all-to-all-start = ((f32[8,1,1024]{2,1,0:T(1,128)}), f32[8,1,1024]{2,1,0:T(1,128)S(1)}, u32[]{:S(2)}, u32[]{:S(2)}) async-start(f32[8,1,1024]{2,1,0:T(1,128)} %reshape.114), calls=%async_computation | async-start | bytes 65536 | tf_op jit(solution)/shard_map/all_to_all | solution.py:31
  64.1 2.9 %all-to-all-done = f32[8,1,1024]{2,1,0:T(1,128)S(1)} async-done(((f32[8,1,1024]{2,1,0:T(1,128)}), f32[8,1,1024]{2,1,0:T(1,128)S(1)}, u32[]{:S(2)}, u32[]{:S(2)}) %all-to-all-start) | async-done | bytes 32800 | tf_op jit(solution)/shard_map/all_to_all | solution.py:31
  67.0 3.4 %all-to-all-start.5 = ((f32[8,1,2048]{2,1,0:T(1,128)}), f32[8,1,2048]{2,1,0:T(1,128)S(1)}, u32[]{:S(2)}, u32[]{:S(2)}) async-start(f32[8,1,2048]{2,1,0:T(1,128)} %reshape.112), calls=%async_computation.5 | async-start | bytes 131072 | tf_op jit(solution)/shard_map/all_to_all | solution.py:49
  72.9 3.1 %all-to-all-done.5 = f32[8,1,2048]{2,1,0:T(1,128)S(1)} async-done(((f32[8,1,2048]{2,1,0:T(1,128)}), f32[8,1,2048]{2,1,0:T(1,128)S(1)}, u32[]{:S(2)}, u32[]{:S(2)}) %all-to-all-start.5) | async-done | bytes 65568 | tf_op jit(solution)/shard_map/all_to_all | solution.py:49
  76.0 3.4 %all-to-all-start.1 = ((f32[8,1,4096]{2,1,0:T(1,128)}), f32[8,1,4096]{2,1,0:T(1,128)S(1)}, u32[]{:S(2)}, u32[]{:S(2)}) async-start(f32[8,1,4096]{2,1,0:T(1,128)} %reshape.116), calls=%async_computation.1 | async-start | bytes 262144 | tf_op jit(solution)/shard_map/all_to_all | solution.py:49
  81.9 3.7 %all-to-all-done.1 = f32[8,1,4096]{2,1,0:T(1,128)S(1)} async-done(((f32[8,1,4096]{2,1,0:T(1,128)}), f32[8,1,4096]{2,1,0:T(1,128)S(1)}, u32[]{:S(2)}, u32[]{:S(2)}) %all-to-all-start.1) | async-done | bytes 131104 | tf_op jit(solution)/shard_map/all_to_all | solution.py:49
  92.9 3.4 %all-to-all-start.2 = ((f32[8,1,2048]{2,1,0:T(1,128)}), f32[8,1,2048]{2,1,0:T(1,128)S(1)}, u32[]{:S(2)}, u32[]{:S(2)}) async-start(f32[8,1,2048]{2,1,0:T(1,128)} %reshape.122), calls=%async_computation.2 | async-start | bytes 131072 | tf_op jit(solution)/shard_map/all_to_all | solution.py:70
  98.3 3.6 %all-to-all-done.2 = f32[8,1,2048]{2,1,0:T(1,128)S(1)} async-done(((f32[8,1,2048]{2,1,0:T(1,128)}), f32[8,1,2048]{2,1,0:T(1,128)S(1)}, u32[]{:S(2)}, u32[]{:S(2)}) %all-to-all-start.2) | async-done | bytes 65568 | tf_op jit(solution)/shard_map/all_to_all | solution.py:70
  101.9 3.6 %all-to-all-start.6 = ((f32[8,1,4096]{2,1,0:T(1,128)}), f32[8,1,4096]{2,1,0:T(1,128)S(1)}, u32[]{:S(2)}, u32[]{:S(2)}) async-start(f32[8,1,4096]{2,1,0:T(1,128)} %reshape.118), calls=%async_computation.6 | async-start | bytes 262144 | tf_op jit(solution)/shard_map/all_to_all | solution.py:70
  108.1 3.4 %all-to-all-done.6 = f32[8,1,4096]{2,1,0:T(1,128)S(1)} async-done(((f32[8,1,4096]{2,1,0:T(1,128)}), f32[8,1,4096]{2,1,0:T(1,128)S(1)}, u32[]{:S(2)}, u32[]{:S(2)}) %all-to-all-start.6) | async-done | bytes 131104 | tf_op jit(solution)/shard_map/all_to_all | solution.py:70
  111.4 3.3 %all-to-all-start.3 = ((f32[8,1,512]{2,1,0:T(1,128)}), f32[8,1,512]{2,1,0:T(1,128)S(1)}, u32[]{:S(2)}, u32[]{:S(2)}) async-start(f32[8,1,512]{2,1,0:T(1,128)} %reshape.124), calls=%async_computation.3 | async-start | bytes 32768 | tf_op jit(solution)/shard_map/all_to_all | solution.py:35
  117.5 2.6 %all-to-all-done.3 = f32[8,1,512]{2,1,0:T(1,128)S(1)} async-done(((f32[8,1,512]{2,1,0:T(1,128)}), f32[8,1,512]{2,1,0:T(1,128)S(1)}, u32[]{:S(2)}, u32[]{:S(2)}) %all-to-all-start.3) | async-done | bytes 16416 | tf_op jit(solution)/shard_map/all_to_all | solution.py:35
  120.2 3.3 %all-to-all-start.7 = ((f32[8,1,1024]{2,1,0:T(1,128)}), f32[8,1,1024]{2,1,0:T(1,128)S(1)}, u32[]{:S(2)}, u32[]{:S(2)}) async-start(f32[8,1,1024]{2,1,0:T(1,128)} %reshape.120), calls=%async_computation.7 | async-start | bytes 65536 | tf_op jit(solution)/shard_map/all_to_all | solution.py:35
  124.4 4.6 %all-to-all-done.7 = f32[8,1,1024]{2,1,0:T(1,128)S(1)} async-done(((f32[8,1,1024]{2,1,0:T(1,128)}), f32[8,1,1024]{2,1,0:T(1,128)S(1)}, u32[]{:S(2)}, u32[]{:S(2)}) %all-to-all-start.7) | async-done | bytes 32800 | tf_op jit(solution)/shard_map/all_to_all | solution.py:35
  130.2 16.5 %all_gather.3 = bf16[128,3,128]{2,0,1:T(8,128)(2,1)S(1)} all-gather(bf16[32,3,128]{2,0,1:T(8,128)(2,1)S(1)} %pad_maximum_fusion.5), channel_id=1, replica_groups=mesh['ctx'=8,'ch'=4] {'ch'}, dimensions={0}, use_global_device_ids=true | all-gather | bytes 122880 | tf_op jit(solution)/shard_map/all_gather | solution.py:130
  146.7 2.2 multiply_bitcast_fusion
  149.6 1.0 copy.182
  151.3 68.0 %reduce-scatter.2.cloned.1.call-done = f32[256,3,128]{0,2,1:T(8,128)} async-done(((f32[2048,3,128]{0,2,1:T(8,128)}), f32[256,3,128]{0,2,1:T(8,128)}) %reduce-scatter.2.cloned.1.call-update) | async-done | bytes 393232 | tf_op jit(solution)/shard_map/reduce_scatter | solution.py:133
  219.3 1.9 copy.183
  (113 shorter events, 32.3 us)
Async XLA Ops:
  7.2 1.4 copy-start
  7.2 3.9 %copy-start.5 = (u32[32]{0:T(128)S(1)}, u32[32]{0:T(128)}, u32[]{:S(2)}) copy-start(u32[32]{0:T(128)} %constant.98) | copy-start | bytes 388
  7.2 5.2 %copy-start.3 = (bf16[32,128]{1,0:T(8,128)(2,1)S(1)}, bf16[32,128]{1,0:T(8,128)(2,1)}, u32[]{:S(2)}) copy-start(bf16[32,128]{1,0:T(8,128)(2,1)} %param.9) | copy-start | bytes 24580
  7.2 5.3 %copy-start.2 = (f32[32,128]{1,0:T(8,128)S(1)}, f32[32,128]{1,0:T(8,128)}, u32[]{:S(2)}) copy-start(f32[32,128]{1,0:T(8,128)} %param.6) | copy-start | bytes 49156
  7.2 36.4 %all-reduce.3.cloned.1.call-start = ((), (), s32[]{:S(2)}) async-start(), calls=%async_computation.10 | async-start | bytes 524288
  47.1 11.0 %all-to-all-start.4 = ((f32[8,1,512]{2,1,0:T(1,128)}), f32[8,1,512]{2,1,0:T(1,128)S(1)}, u32[]{:S(2)}, u32[]{:S(2)}) async-start(f32[8,1,512]{2,1,0:T(1,128)} %reshape.110), calls=%async_computation.4 | async-start | bytes 32768 | tf_op jit(solution)/shard_map/all_to_all | solution.py:31
  58.2 8.8 %all-to-all-start = ((f32[8,1,1024]{2,1,0:T(1,128)}), f32[8,1,1024]{2,1,0:T(1,128)S(1)}, u32[]{:S(2)}, u32[]{:S(2)}) async-start(f32[8,1,1024]{2,1,0:T(1,128)} %reshape.114), calls=%async_computation | async-start | bytes 65536 | tf_op jit(solution)/shard_map/all_to_all | solution.py:31
  67.0 9.1 %all-to-all-start.5 = ((f32[8,1,2048]{2,1,0:T(1,128)}), f32[8,1,2048]{2,1,0:T(1,128)S(1)}, u32[]{:S(2)}, u32[]{:S(2)}) async-start(f32[8,1,2048]{2,1,0:T(1,128)} %reshape.112), calls=%async_computation.5 | async-start | bytes 131072 | tf_op jit(solution)/shard_map/all_to_all | solution.py:49
  76.0 9.5 %all-to-all-start.1 = ((f32[8,1,4096]{2,1,0:T(1,128)}), f32[8,1,4096]{2,1,0:T(1,128)S(1)}, u32[]{:S(2)}, u32[]{:S(2)}) async-start(f32[8,1,4096]{2,1,0:T(1,128)} %reshape.116), calls=%async_computation.1 | async-start | bytes 262144 | tf_op jit(solution)/shard_map/all_to_all | solution.py:49
  92.9 9.1 %all-to-all-start.2 = ((f32[8,1,2048]{2,1,0:T(1,128)}), f32[8,1,2048]{2,1,0:T(1,128)S(1)}, u32[]{:S(2)}, u32[]{:S(2)}) async-start(f32[8,1,2048]{2,1,0:T(1,128)} %reshape.122), calls=%async_computation.2 | async-start | bytes 131072 | tf_op jit(solution)/shard_map/all_to_all | solution.py:70
  101.9 9.5 %all-to-all-start.6 = ((f32[8,1,4096]{2,1,0:T(1,128)}), f32[8,1,4096]{2,1,0:T(1,128)S(1)}, u32[]{:S(2)}, u32[]{:S(2)}) async-start(f32[8,1,4096]{2,1,0:T(1,128)} %reshape.118), calls=%async_computation.6 | async-start | bytes 262144 | tf_op jit(solution)/shard_map/all_to_all | solution.py:70
  111.4 8.7 %all-to-all-start.3 = ((f32[8,1,512]{2,1,0:T(1,128)}), f32[8,1,512]{2,1,0:T(1,128)S(1)}, u32[]{:S(2)}, u32[]{:S(2)}) async-start(f32[8,1,512]{2,1,0:T(1,128)} %reshape.124), calls=%async_computation.3 | async-start | bytes 32768 | tf_op jit(solution)/shard_map/all_to_all | solution.py:35
  116.0 13.9 %copy-start.4 = (f32[32]{0:T(128)S(1)}, f32[32]{0:T(128)}, u32[]{:S(2)}) copy-start(f32[32]{0:T(128)} %param.8) | copy-start | bytes 388
  116.1 30.7 %copy-start.1 = (bf16[2048,128]{1,0:T(8,128)(2,1)S(1)}, bf16[2048,128]{1,0:T(8,128)(2,1)}, u32[]{:S(2)}) copy-start(bf16[2048,128]{1,0:T(8,128)(2,1)} %param.5) | copy-start | bytes 1572868
  120.2 8.8 %all-to-all-start.7 = ((f32[8,1,1024]{2,1,0:T(1,128)}), f32[8,1,1024]{2,1,0:T(1,128)S(1)}, u32[]{:S(2)}, u32[]{:S(2)}) async-start(f32[8,1,1024]{2,1,0:T(1,128)} %reshape.120), calls=%async_computation.7 | async-start | bytes 65536 | tf_op jit(solution)/shard_map/all_to_all | solution.py:35
  123.5 95.8 %reduce-scatter.2.cloned.1.call-start = ((), (), s32[]{:S(2)}) async-start(), calls=%async_computation.9 | async-start | bytes 3538944 | tf_op jit(solution)/shard_map/reduce_scatter | solution.py:133
Sparse Core Ops, SparseCore 0:
  11.1 32.5 all-reduce.2
  149.1 70.1 reduce-scatter.1
where the time goes:
time: 230 us; the launch traced here: 228 us
  waiting for transfers between devices  127 us (55%)
  starting transfers between devices  29.3 us (13%)
  local copies, waits for them, and re-layouts  17 us (7%)
  blocking collectives  16.5 us (7%)
  between operations  15.4 us (7%)
  matrix products  14.2 us (6%)
  other arithmetic  9.06 us (4%)
    reduce_scatter x1, waiting for transfers between devices, shards(): lax.psum_scatter(jnp.einsum('il,ojl->ijo', piece, all_grads, preferred_el...  68 us
    unnamed x3, waiting for transfers between devices  31 us
    all_gather x1, blocking collectives, shards(): all_grads = lax.all_gather(grad_proj, 'ch', axis=0, tiled=True)  16.5 us
    unnamed x38, local copies, waits for them, and re-layouts  14 us
    all_to_all x2, starting transfers between devices, spread(): lax.all_to_all(fields[:, None, :], 'ctx', split_axis=2, concat_axis=1, ti...  8.95 us
    all_to_all x2, waiting for transfers between devices, gather_back(): lax.all_to_all(parted, 'ctx', split_axis=1, concat_axis=2, tiled=True)  7.25 us
    all_to_all x2, waiting for transfers between devices, unspectrum(): lax.all_to_all(jnp.stack([real_part, imag_part]), 'ctx', split_axis=3, co...  7.01 us
    all_to_all x2, starting transfers between devices, unspectrum(): lax.all_to_all(jnp.stack([real_part, imag_part]), 'ctx', split_axis=3, co...  6.9 us
  transfers between devices with their start and end apart: 10, of which 10 were waited for; matrix products, arithmetic and copies ran while one was open for 9% of the time, Pallas kernels for 0%

commit v1 on v0

--- a/solution.py
+++ b/solution.py
@@ -1,8 +1,11 @@
+import functools
 import math
 
 import jax
 import jax.numpy as jnp
 from jax import lax
+from jax.experimental import pallas as pl
+from jax.experimental.pallas import tpu as pltpu
 from jax.sharding import PartitionSpec as P
 
 highest = lax.Precision.HIGHEST
@@ -142,7 +145,318 @@
     return (input_grad.astype(jnp.bfloat16), weight_grad, grad_filter * scale)
 
 
+MESH = pl.DeviceIdType.MESH
+PER_OWNER = 4
+
+
+def toeplitz(row, put):
+    lanes = row.shape[1]
+    keep = lax.broadcasted_iota(jnp.int32, (lanes, lanes), 1) >= lax.broadcasted_iota(
+        jnp.int32, (lanes, lanes), 0
+    )
+    before = jnp.zeros((lanes, lanes), jnp.float32)
+    for d in range(row.shape[0]):
+        turned = pltpu.roll(
+            jnp.broadcast_to(row[d : d + 1], (lanes, lanes)), 0, 1, stride=1, stride_axis=0
+        )
+        put(d, jnp.where(keep, turned, before).astype(jnp.bfloat16))
+        before = turned
+
+
+def shifted(block, down):
+    rows = block.shape[0]
+    place = lax.broadcasted_iota(jnp.int32, block.shape, 0)
+    parts = []
+    for d in range(rows):
+        if d == 0:
+            parts.append(block)
+        elif down:
+            parts.append(jnp.where(place >= d, pltpu.roll(block, d, 0), 0.0))
+        else:
+            parts.append(jnp.where(place < rows - d, pltpu.roll(block, rows - d, 0), 0.0))
+    return jnp.concatenate(parts, axis=1).astype(jnp.bfloat16)
+
+
+def fused(
+    n, m, scale,
+    x_hbm, f_ref, w_hbm, gain_ref, cot_ref,
+    gx_ref, gw_ref, gf_ref,
+    xv, wv, xall, cot32, fsend, fall, part, psend, precv, csum, csend, call,
+    tcat, tvert, gall, gf32, gmat, fgs, fgall,
+    lsem, xs, xr, fs, fr, ps, pr, cs, cr, hs, hr, gs, gr,
+):
+    k = lax.axis_index("ctx")
+    h = lax.axis_index("ch")
+    chans = f_ref.shape[0]
+    width = f_ref.shape[1]
+    rows = xall.shape[0]
+    core_h = h + 1 - 2 * lax.rem(h, 2)
+    y_h = lax.rem(h + 2, m)
+    diag_h = lax.rem(core_h + 2, m)
+    bf16, f32 = jnp.bfloat16, jnp.float32
+
+    def remote(src, dst, send, recv, kk, hh):
+        return pltpu.make_async_remote_copy(
+            src_ref=src, dst_ref=dst, send_sem=send, recv_sem=recv,
+            device_id=(kk, hh), device_id_type=MESH,
+        )
+
+    load_x = pltpu.make_async_copy(x_hbm, xv, lsem.at[0])
+    load_x.start()
+    load_w = [
+        pltpu.make_async_copy(w_hbm.at[j], wv.at[:, pl.ds(j * 128, 128)], lsem.at[1 + j])
+        for j in range(3)
+    ]
+    for copy in load_w:
+        copy.start()
+    own_x = pltpu.make_async_copy(
+        x_hbm.at[pl.ds(pl.multiple_of(k * rows, rows), rows), :],
+        xall.at[:, pl.ds(pl.multiple_of(k * width, width), width)],
+        lsem.at[4],
+    )
+    own_x.start()
+
+    barrier = pltpu.get_barrier_semaphore()
+    for i in range(1, n):
+        pl.semaphore_signal(barrier, 1, device_id=(lax.rem(k + i, n), h), device_id_type=MESH)
+    for i in range(1, m):
+        pl.semaphore_signal(barrier, 1, device_id=(k, lax.rem(h + i, m)), device_id_type=MESH)
+
+    cot32[...] = cot_ref[...].astype(f32)
+    for q in range(n):
+        fsend[q, 0:4, :] = f_ref[pl.ds(q, PER_OWNER, stride=n), :]
+        fsend[q, 4:8, :] = cot32[pl.ds(q, PER_OWNER, stride=n), :]
+    fall[k] = fsend[k]
+    pl.semaphore_wait(barrier, n + m - 2)
+
+    sends = []
+    for i in range(1, n):
+        kk = lax.rem(k + i, n)
+        copy = remote(fsend.at[kk], fall.at[k], fs.at[i], fr.at[k], kk, h)
+        copy.start()
+        sends.append(copy)
+    for i in range(1, n):
+        kk = lax.rem(k + i, n)
+        copy = remote(
+            x_hbm.at[pl.ds(pl.multiple_of(kk * rows, rows), rows), :],
+            xall.at[:, pl.ds(pl.multiple_of(k * width, width), width)],
+            xs.at[i], xr.at[k], kk, h,
+        )
+        copy.start()
+        sends.append(copy)
+
+    load_x.wait()
+    for copy in load_w:
+        copy.wait()
+    turned = jnp.dot(xv[...].T, wv[...], preferred_element_type=f32)
+    for j in range(3):
+        piece = turned[:, j * 128 : (j + 1) * 128].T
+        for q in range(m):
+            cut = piece[q * chans : (q + 1) * chans]
+            part[q, j * chans : (j + 1) * chans, :] = cut
+            psend[q, j * chans : (j + 1) * chans, :] = cut.astype(bf16)
+    for i in range(1, m):
+        hh = lax.rem(h + i, m)
+        copy = remote(psend.at[hh], precv.at[h], ps.at[i], pr.at[h], k, hh)
+        copy.start()
+        sends.append(copy)
+
+    for i in range(1, n):
+        kk = lax.rem(k + n - i, n)
+        remote(fsend.at[kk], fall.at[kk], fs.at[i], fr.at[kk], kk, h).wait_recv()
+    for c in range(PER_OWNER):
+        def put_f(d, tile, c=c):
+            tcat[c, 0:128, d * 128 : (d + 1) * 128] = tile
+            tvert[c, d * 128 : (d + 1) * 128, :] = tile
+        toeplitz(fall[:, c, :], put_f)
+
+    total = part[h]
+    for i in range(1, m):
+        hh = lax.rem(h + m - i, m)
+        remote(psend.at[hh], precv.at[hh], ps.at[i], pr.at[hh], k, hh).wait_recv()
+        total = total + precv[hh].astype(f32)
+    csum[...] = total
+    for q in range(n):
+        csend[q] = csum[pl.ds(q, 3 * PER_OWNER, stride=n), :]
+    call[k] = csend[k]
+    for i in range(1, n):
+        kk = lax.rem(k + i, n)
+        copy = remote(csend.at[kk], call.at[k], cs.at[i], cr.at[k], kk, h)
+        copy.start()
+        sends.append(copy)
+    for i in range(1, n):
+        kk = lax.rem(k + n - i, n)
+        remote(csend.at[kk], call.at[kk], cs.at[i], cr.at[kk], kk, h).wait_recv()
+
+    me = h * n + k
+    made = []
+    for c in range(PER_OWNER):
+        outer = call[:, c, :]
+        inner = call[:, PER_OWNER + c, :]
+        value = call[:, 2 * PER_OWNER + c, :]
+        grad_out = fall[:, PER_OWNER + c, :]
+        gain = gain_ref[c * n + k]
+        product = inner * value
+        grad_mixed = grad_out * outer
+
+        def put_p(d, tile, c=c):
+            tcat[c, 128:256, d * 128 : (d + 1) * 128] = tile
+        toeplitz(product, put_p)
+        convolved = jnp.dot(shifted(product, True), tvert[c], preferred_element_type=f32)
+        both = lax.dot_general(
+            shifted(grad_mixed, False), tcat[c], (((1,), (1,)), ((), ())),
+            preferred_element_type=f32,
+        )
+        grad_product = both[:, :128] + gain * grad_mixed
+        fgs[:, c, :] = both[:, 128:] * scale
+        made.append(
+            (grad_out * (convolved + gain * product), grad_product * value, grad_product * inner)
+        )
+    for j in range(3):
+        for c in range(0, PER_OWNER, 2):
+            gall[me, j * chans + c * n : j * chans + (c + 2) * n, :] = jnp.concatenate(
+                [made[c][j], made[c + 1][j]], axis=0
+            ).astype(bf16)
+
+    count = 0
+
+    def push(slot, kk, hh, index):
+        copy = remote(gall.at[slot], gall.at[slot], gs.at[index], gr.at[slot], kk, hh)
+        copy.start()
+        sends.append(copy)
+
+    def landed(slot):
+        remote(gall.at[slot], gall.at[slot], gs.at[0], gr.at[slot], k, y_h).wait_recv()
+
+    for i in range(1, n):
+        push(me, lax.rem(k + i, n), h, count)
+        count += 1
+    push(me, k, y_h, count)
+    push(me, k, core_h, count + 1)
+    count += 2
+    fgall[k] = fgs[k]
+    for i in range(1, n):
+        kk = lax.rem(k + i, n)
+        copy = remote(fgs.at[kk], fgall.at[k], hs.at[i], hr.at[k], kk, h)
+        copy.start()
+        sends.append(copy)
+    for i in range(1, n):
+        slot = h * n + lax.rem(k + n - i, n)
+        landed(slot)
+        push(slot, k, y_h, count)
+        push(slot, k, core_h, count + 1)
+        count += 2
+    for i in range(n):
+        slot = y_h * n + lax.rem(k + n - i, n)
+        landed(slot)
+        push(slot, k, core_h, count)
+        count += 1
+    for i in range(1, n):
+        kk = lax.rem(k + n - i, n)
+        remote(fgs.at[kk], fgall.at[kk], hs.at[i], hr.at[kk], kk, h).wait_recv()
+    for c in range(PER_OWNER):
+        gf_ref[c * n : (c + 1) * n, :] = fgall[:, c, :]
+    own_x.wait()
+    for i in range(1, n):
+        kk = lax.rem(k + n - i, n)
+        remote(
+            x_hbm.at[pl.ds(pl.multiple_of(kk * rows, rows), rows), :],
+            xall.at[:, pl.ds(pl.multiple_of(kk * width, width), width)],
+            xs.at[i], xr.at[kk], kk, h,
+        ).wait_recv()
+    for i in range(n):
+        for hh in (core_h, diag_h):
+            landed(hh * n + lax.rem(k + n - i, n))
+
+    block = 3 * chans
+    for q in range(m * n):
+        gf32[q * block : (q + 1) * block, :] = gall[q].astype(f32)
+    for hh in range(m):
+        for j in range(3):
+            for c in range(0, PER_OWNER, 2):
+                for b in range(n):
+                    pair = [
+                        gf32[pl.ds(hh * n * block + j * chans + cc * n + b, n, stride=block), :]
+                        for cc in (c, c + 1)
+                    ]
+                    start = j * 128 + hh * chans + c * n
+                    gmat[start : start + 2 * n, b * 128 : (b + 1) * 128] = jnp.concatenate(
+                        pair, axis=0
+                    ).astype(bf16)
+    here = gmat[:, pl.ds(pl.multiple_of(k * width, width), width)]
+    gx_ref[...] = jnp.dot(wv[...], here, preferred_element_type=f32).astype(bf16)
+    wide = lax.dot_general(
+        xall[...], gmat[...], (((1,), (1,)), ((), ())), preferred_element_type=f32
+    ) * scale
+    for j in range(3):
+        gw_ref[j] = wide[:, j * 128 : (j + 1) * 128]
+    for copy in sends:
+        copy.wait_send()
+
+
+def fused_shards(n, m, x_slab, filter_taps, mix_weight, skip_gain, cotangent):
+    depth, width = x_slab.shape
+    chans = cotangent.shape[0]
+    rows = depth // n
+    total = chans * m
+    bf16, f32 = jnp.bfloat16, jnp.float32
+    scale = 1.0 / math.sqrt(n * width)
+    dma = pltpu.SemaphoreType.DMA
+    vmem = pl.BlockSpec(memory_space=pltpu.VMEM)
+    anywhere = pl.BlockSpec(memory_space=pl.ANY)
+    gx, gw, gf = pl.pallas_call(
+        functools.partial(fused, n, m, scale),
+        out_shape=(
+            jax.ShapeDtypeStruct((depth, width), bf16),
+            jax.ShapeDtypeStruct((3, rows, total), f32),
+            jax.ShapeDtypeStruct((chans, width), f32),
+        ),
+        in_specs=[anywhere, vmem, anywhere, pl.BlockSpec(memory_space=pltpu.SMEM), vmem],
+        out_specs=(vmem, vmem, vmem),
+        scratch_shapes=[
+            pltpu.VMEM((depth, width), bf16),
+            pltpu.VMEM((depth, 3 * total), bf16),
+            pltpu.VMEM((rows, n * width), bf16),
+            pltpu.VMEM((chans, width), f32),
+            pltpu.VMEM((n, 2 * PER_OWNER, width), f32),
+            pltpu.VMEM((n, 2 * PER_OWNER, width), f32),
+            pltpu.VMEM((m, 3 * chans, width), f32),
+            pltpu.VMEM((m, 3 * chans, width), bf16),
+            pltpu.VMEM((m, 3 * chans, width), bf16),
+            pltpu.VMEM((3 * chans, width), f32),
+            pltpu.VMEM((n, 3 * PER_OWNER, width), f32),
+            pltpu.VMEM((n, 3 * PER_OWNER, width), f32),
+            pltpu.VMEM((PER_OWNER, 2 * width, n * width), bf16),
+            pltpu.VMEM((PER_OWNER, n * width, width), bf16),
+            pltpu.VMEM((m * n, 3 * chans, width), bf16),
+            pltpu.VMEM((m * n * 3 * chans, width), f32),
+            pltpu.VMEM((3 * total, n * width), bf16),
+            pltpu.VMEM((n, PER_OWNER, width), f32),
+            pltpu.VMEM((n, PER_OWNER, width), f32),
+            dma((5,)),
+            dma((n,)), dma((n,)),
+            dma((n,)), dma((n,)),
+            dma((m,)), dma((m,)),
+            dma((n,)), dma((n,)),
+            dma((n,)), dma((n,)),
+            dma((n + 1 + 2 * (n - 1) + n,)), dma((m * n,)),
+        ],
+        compiler_params=pltpu.CompilerParams(
+            collective_id=0, has_side_effects=True, vmem_limit_bytes=40 * 1024 * 1024
+        ),
+    )(x_slab, filter_taps, jnp.transpose(mix_weight, (1, 0, 2)), skip_gain, cotangent)
+    return (gx, jnp.transpose(gw, (1, 0, 2)), gf)
+
+
 def solution(mesh):
+    n, m = mesh.shape["ctx"], mesh.shape["ch"]
+
+    def body(x_slab, filter_taps, mix_weight, skip_gain, cotangent):
+        chans, width = cotangent.shape
+        if chans == PER_OWNER * n and width == 128 and n == 8 and m == 4:
+            return fused_shards(n, m, x_slab, filter_taps, mix_weight, skip_gain, cotangent)
+        return shards(x_slab, filter_taps, mix_weight, skip_gain, cotangent)
+
     in_specs = (P("ch", "ctx"), P("ch", "ctx"), P("ch", None, None), P("ch"), P("ch", "ctx"))
     out_specs = (P("ch", "ctx"), P(("ch", "ctx"), None, None), P("ch", "ctx"))
-    return jax.shard_map(shards, mesh=mesh, in_specs=in_specs, out_specs=out_specs, check_vma=False)
+    return jax.shard_map(body, mesh=mesh, in_specs=in_specs, out_specs=out_specs, check_vma=False)

time: 230 us -> 43.3 us (0.19)
  waiting for transfers between devices: 127 us -> 0 us
  Pallas kernels: 0 us -> 35.7 us
  starting transfers between devices: 29.3 us -> 0 us
  blocking collectives: 16.5 us -> 0 us
  between operations: 15.4 us -> 0.65 us
  matrix products: 14.2 us -> 0 us
  local copies, waits for them, and re-layouts: 17 us -> 6.66 us
  other arithmetic: 9.06 us -> 0 us
    reduce_scatter x1 -> x0, waiting for transfers between devices: 68 us -> none  [shards(): lax.psum_scatter(jnp.einsum('il,ojl->ijo', piece, all_grads, preferred_el...]
    pallas_call x0 -> x1, Pallas kernels: none -> 35.7 us  [fused_shards(): pl.pallas_call(functools.partial(fused, n, m, scale), out_shape=(jax.Shap...]
    unnamed x3 -> x0, waiting for transfers between devices: 31 us -> none
    all_to_all x8 -> x0, starting transfers between devices: 29.3 us -> none  [the longest x2 8.95 us: spread(): lax.all_to_all(fields[:, None, :], 'ctx', split_axis=2, concat_axis=1, ti...]
    all_to_all x8 -> x0, waiting for transfers between devices: 27.7 us -> none  [the longest x2 7.25 us: gather_back(): lax.all_to_all(parted, 'ctx', split_axis=1, concat_axis=2, tiled=True)]
    all_gather x1 -> x0, blocking collectives: 16.5 us -> none  [shards(): all_grads = lax.all_gather(grad_proj, 'ch', axis=0, tiled=True)]
    dot_general x27 -> x0, matrix products: 14.2 us -> none  [the longest x1 2.23 us: shards(): jnp.einsum('il,ojl->ijo', piece, all_grads, preferred_element_type=jnp.fl...]
    unnamed x38 -> x13, local copies, waits for them, and re-layouts: 14 us -> 6.66 us
  transfers between devices with their start and end apart: 10 -> 0, of which waited for: 10 -> 0; matrix products, arithmetic and copies ran while one was open for 9% -> 0% of each run, Pallas kernels for 0% -> 0%
where the time goes in v1:
time: 43.3 us; the launch traced here: 43 us
  Pallas kernels  35.7 us (82%)
  local copies, waits for them, and re-layouts  6.66 us (15%)
  between operations  0.65 us (2%)
    pallas_call x1, Pallas kernels, fused_shards(): pl.pallas_call(functools.partial(fused, n, m, scale), out_shape=(jax.Shap...  35.7 us
    unnamed x13, local copies, waits for them, and re-layouts  6.66 us

profile of v1, /device:TPU:1, one launch (start us, length us, event | category | flops | bytes accessed | tf_op | source)
XLA Modules:
  0.0 43.0 jit_solution(12417494484879308806)
XLA Ops:
  0.6 0.0 copy-start
  0.6 1.4 %copy-done = bf16[2048,3,128]{2,0,1:T(8,128)(2,1)S(1)} copy-done((bf16[2048,3,128]{2,0,1:T(8,128)(2,1)S(1)}, bf16[2048,3,128]{2,0,1:T(8,128)(2,1)}, u32[]{:S(2)}) %copy-start) | copy-done | bytes 1572888
  2.0 0.0 copy-start.1
  2.0 1.0 %copy-done.1 = bf16[2048,128]{1,0:T(8,128)(2,1)S(1)} copy-done((bf16[2048,128]{1,0:T(8,128)(2,1)S(1)}, bf16[2048,128]{1,0:T(8,128)(2,1)}, u32[]{:S(2)}) %copy-start.1) | copy-done | bytes 524312
  3.1 0.0 copy-start.2
  3.1 0.7 %copy-done.2 = f32[32,128]{1,0:T(8,128)S(1)} copy-done((f32[32,128]{1,0:T(8,128)S(1)}, f32[32,128]{1,0:T(8,128)}, u32[]{:S(2)}) %copy-start.2) | copy-done | bytes 16408
  3.8 0.0 copy-start.3
  3.8 0.7 %copy-done.3 = bf16[32,128]{1,0:T(8,128)(2,1)S(1)} copy-done((bf16[32,128]{1,0:T(8,128)(2,1)S(1)}, bf16[32,128]{1,0:T(8,128)(2,1)}, u32[]{:S(2)}) %copy-start.3) | copy-done | bytes 8216
  4.5 0.0 copy-start.4
  4.5 0.7 %copy-done.4 = f32[32]{0:T(128)S(1)} copy-done((f32[32]{0:T(128)S(1)}, f32[32]{0:T(128)}, u32[]{:S(2)}) %copy-start.4) | copy-done | bytes 152
  5.2 35.7 %shard_map.76 = (bf16[2048,128]{1,0:T(8,128)(2,1)S(1)}, f32[3,256,128]{2,1,0:T(8,128)S(1)}, f32[32,128]{1,0:T(8,128)S(1)}) custom-call(bf16[2048,128]{1,0:T(8,128)(2,1)S(1)} %copy-done.1, f32[32,128]{1,0:T(8,128)S(1)} %copy-done.2, bf16[3,2048,128]{2,1,0:T(8,128)(2,1)S(1)} %bitcast.2, f32[32]{0:T(128)S(1)} %copy-done.4, bf16[32,128]{1,0:T(8,128)(2,1)S(1)} %copy-done.3), custom_call_target="tpu_custom_call" | custom-call | tf_op jit(solution)/shard_map/pallas_call | solution.py:407
  40.8 0.8 %copy.11 = bf16[2048,128]{1,0:T(8,128)(2,1)} copy(bf16[2048,128]{1,0:T(8,128)(2,1)S(1)} %get-tuple-element.12) | data formatting | bytes 1048576
  41.6 0.7 %copy.12 = f32[256,3,128]{2,0,1:T(8,128)} copy(f32[256,3,128]{2,0,1:T(8,128)S(1)} %bitcast.3) | data formatting | bytes 786432
  42.4 0.6 %copy.13 = f32[32,128]{1,0:T(8,128)} copy(f32[32,128]{1,0:T(8,128)S(1)} %get-tuple-element.14) | data formatting | bytes 32768
Async XLA Ops:
  0.6 1.4 %copy-start = (bf16[2048,3,128]{2,0,1:T(8,128)(2,1)S(1)}, bf16[2048,3,128]{2,0,1:T(8,128)(2,1)}, u32[]{:S(2)}) copy-start(bf16[2048,3,128]{2,0,1:T(8,128)(2,1)} %param.7) | copy-start | bytes 4718596
  2.0 1.0 %copy-start.1 = (bf16[2048,128]{1,0:T(8,128)(2,1)S(1)}, bf16[2048,128]{1,0:T(8,128)(2,1)}, u32[]{:S(2)}) copy-start(bf16[2048,128]{1,0:T(8,128)(2,1)} %x_hbm.1) | copy-start | bytes 1572868
  3.1 0.7 %copy-start.2 = (f32[32,128]{1,0:T(8,128)S(1)}, f32[32,128]{1,0:T(8,128)}, u32[]{:S(2)}) copy-start(f32[32,128]{1,0:T(8,128)} %f_ref.1) | copy-start | bytes 49156
  3.8 0.7 %copy-start.3 = (bf16[32,128]{1,0:T(8,128)(2,1)S(1)}, bf16[32,128]{1,0:T(8,128)(2,1)}, u32[]{:S(2)}) copy-start(bf16[32,128]{1,0:T(8,128)(2,1)} %cot_ref.1) | copy-start | bytes 24580
  4.5 0.7 %copy-start.4 = (f32[32]{0:T(128)S(1)}, f32[32]{0:T(128)}, u32[]{:S(2)}) copy-start(f32[32]{0:T(128)} %gain_ref.1) | copy-start | bytes 388

commit v2 on v1

--- a/solution.py
+++ b/solution.py
@@ -147,6 +147,7 @@
 
 MESH = pl.DeviceIdType.MESH
 PER_OWNER = 4
+CUTS = (0, 6, 10, 16)
 
 
 def toeplitz(row, put):
@@ -179,10 +180,10 @@
 
 def fused(
     n, m, scale,
-    x_hbm, f_ref, w_hbm, gain_ref, cot_ref,
-    gx_ref, gw_ref, gf_ref,
-    xv, wv, xall, cot32, fsend, fall, part, psend, precv, csum, csend, call,
-    tcat, tvert, gall, gf32, gmat, fgs, fgall,
+    x_hbm, f_hbm, w_hbm, gain_hbm, cot_hbm,
+    gmat, xall, gf_ref,
+    f_ref, cot_ref, gain_ref, xv, wv, cot32, fsend, fall, part, psend, precv, csum, csend, call,
+    tcat, tvert, gall, gf32, fgs, fgall,
     lsem, xs, xr, fs, fr, ps, pr, cs, cr, hs, hr, gs, gr,
 ):
     k = lax.axis_index("ctx")
@@ -190,6 +191,9 @@
     chans = f_ref.shape[0]
     width = f_ref.shape[1]
     rows = xall.shape[0]
+    cuts = [rows * c // 16 for c in CUTS]
+    pieces = [(a, b - a) for a, b in zip(cuts[:-1], cuts[1:])]
+    sends = []
     core_h = h + 1 - 2 * lax.rem(h, 2)
     y_h = lax.rem(h + 2, m)
     diag_h = lax.rem(core_h + 2, m)
@@ -201,20 +205,44 @@
             device_id=(kk, hh), device_id_type=MESH,
         )
 
+    def x_copy(i, part_of, source, target):
+        start, size = pieces[part_of]
+        return remote(
+            x_hbm.at[pl.ds(pl.multiple_of(target * rows + start, 16), size), :],
+            xall.at[pl.ds(start, size), pl.ds(pl.multiple_of(source * width, width), width)],
+            xs.at[part_of * n + i], xr.at[part_of * n + source], target, h,
+        )
+
+    def wait_x(i, part_of, source):
+        start, size = pieces[part_of]
+        block = xall.at[pl.ds(start, size), pl.ds(pl.multiple_of(source * width, width), width)]
+        remote(
+            block, block, xs.at[part_of * n + i], xr.at[part_of * n + source], source, h
+        ).wait_recv()
+
+    def send_x(part_of):
+        for i in range(1, n):
+            copy = x_copy(i, part_of, k, lax.rem(k + i, n))
+            copy.start()
+            sends.append(copy)
+
     load_x = pltpu.make_async_copy(x_hbm, xv, lsem.at[0])
-    load_x.start()
     load_w = [
         pltpu.make_async_copy(w_hbm.at[j], wv.at[:, pl.ds(j * 128, 128)], lsem.at[1 + j])
         for j in range(3)
     ]
-    for copy in load_w:
-        copy.start()
+    load_small = [
+        pltpu.make_async_copy(f_hbm, f_ref, lsem.at[5]),
+        pltpu.make_async_copy(cot_hbm, cot_ref, lsem.at[6]),
+        pltpu.make_async_copy(gain_hbm, gain_ref, lsem.at[7]),
+    ]
     own_x = pltpu.make_async_copy(
         x_hbm.at[pl.ds(pl.multiple_of(k * rows, rows), rows), :],
         xall.at[:, pl.ds(pl.multiple_of(k * width, width), width)],
         lsem.at[4],
     )
-    own_x.start()
+    for copy in load_small + [load_x] + load_w + [own_x]:
+        copy.start()
 
     barrier = pltpu.get_barrier_semaphore()
     for i in range(1, n):
@@ -222,6 +250,8 @@
     for i in range(1, m):
         pl.semaphore_signal(barrier, 1, device_id=(k, lax.rem(h + i, m)), device_id_type=MESH)
 
+    for copy in load_small:
+        copy.wait()
     cot32[...] = cot_ref[...].astype(f32)
     for q in range(n):
         fsend[q, 0:4, :] = f_ref[pl.ds(q, PER_OWNER, stride=n), :]
@@ -229,21 +259,12 @@
     fall[k] = fsend[k]
     pl.semaphore_wait(barrier, n + m - 2)
 
-    sends = []
     for i in range(1, n):
         kk = lax.rem(k + i, n)
         copy = remote(fsend.at[kk], fall.at[k], fs.at[i], fr.at[k], kk, h)
         copy.start()
         sends.append(copy)
-    for i in range(1, n):
-        kk = lax.rem(k + i, n)
-        copy = remote(
-            x_hbm.at[pl.ds(pl.multiple_of(kk * rows, rows), rows), :],
-            xall.at[:, pl.ds(pl.multiple_of(k * width, width), width)],
-            xs.at[i], xr.at[k], kk, h,
-        )
-        copy.start()
-        sends.append(copy)
+    send_x(0)
 
     load_x.wait()
     for copy in load_w:
@@ -284,6 +305,7 @@
         copy = remote(csend.at[kk], call.at[k], cs.at[i], cr.at[k], kk, h)
         copy.start()
         sends.append(copy)
+    send_x(1)
     for i in range(1, n):
         kk = lax.rem(k + n - i, n)
         remote(csend.at[kk], call.at[kk], cs.at[i], cr.at[kk], kk, h).wait_recv()
@@ -334,6 +356,7 @@
     push(me, k, y_h, count)
     push(me, k, core_h, count + 1)
     count += 2
+    send_x(2)
     fgall[k] = fgs[k]
     for i in range(1, n):
         kk = lax.rem(k + i, n)
@@ -359,11 +382,8 @@
     own_x.wait()
     for i in range(1, n):
         kk = lax.rem(k + n - i, n)
-        remote(
-            x_hbm.at[pl.ds(pl.multiple_of(kk * rows, rows), rows), :],
-            xall.at[:, pl.ds(pl.multiple_of(kk * width, width), width)],
-            xs.at[i], xr.at[kk], kk, h,
-        ).wait_recv()
+        for part_of in range(3):
+            wait_x(i, part_of, kk)
     for i in range(n):
         for hh in (core_h, diag_h):
             landed(hh * n + lax.rem(k + n - i, n))
@@ -383,15 +403,60 @@
                     gmat[start : start + 2 * n, b * 128 : (b + 1) * 128] = jnp.concatenate(
                         pair, axis=0
                     ).astype(bf16)
-    here = gmat[:, pl.ds(pl.multiple_of(k * width, width), width)]
-    gx_ref[...] = jnp.dot(wv[...], here, preferred_element_type=f32).astype(bf16)
-    wide = lax.dot_general(
-        xall[...], gmat[...], (((1,), (1,)), ((), ())), preferred_element_type=f32
-    ) * scale
-    for j in range(3):
-        gw_ref[j] = wide[:, j * 128 : (j + 1) * 128]
     for copy in sends:
         copy.wait_send()
+
+
+def finish(
+    parts, scale, g_hbm, x_hbm, w_hbm, f_hbm, gx_hbm, gw_hbm, gf_hbm,
+    gv, xv, wv, fv, gx, gw, lsem, wsem, osem,
+):
+    k = lax.axis_index("ctx")
+    depth, width = gx.shape
+    total = gw.shape[2]
+    step = depth // parts
+    load_g = pltpu.make_async_copy(g_hbm, gv, lsem.at[0])
+    load_x = pltpu.make_async_copy(x_hbm, xv, lsem.at[1])
+    load_f = pltpu.make_async_copy(f_hbm, fv, lsem.at[2])
+    load_w = [
+        pltpu.make_async_copy(
+            w_hbm.at[j, pl.ds(p * step, step), :],
+            wv.at[pl.ds(p * step, step), pl.ds(j * total, total)],
+            wsem.at[p * 3 + j],
+        )
+        for p in range(parts)
+        for j in range(3)
+    ]
+    for copy in [load_g, load_x] + load_w + [load_f]:
+        copy.start()
+    stores = []
+    load_g.wait()
+    load_x.wait()
+    for j in range(3):
+        gw[j] = lax.dot_general(
+            xv[...], gv[j * total : (j + 1) * total, :], (((1,), (1,)), ((), ())),
+            preferred_element_type=jnp.float32,
+        ) * scale
+        copy = pltpu.make_async_copy(gw.at[j], gw_hbm.at[j], osem.at[j])
+        copy.start()
+        stores.append(copy)
+    here = gv[:, pl.ds(pl.multiple_of(k * width, width), width)]
+    for p in range(parts):
+        for j in range(3):
+            load_w[p * 3 + j].wait()
+        span = pl.ds(p * step, step)
+        gx[span, :] = jnp.dot(wv[span, :], here, preferred_element_type=jnp.float32).astype(
+            jnp.bfloat16
+        )
+        copy = pltpu.make_async_copy(gx.at[span, :], gx_hbm.at[span, :], osem.at[3 + p])
+        copy.start()
+        stores.append(copy)
+    load_f.wait()
+    copy = pltpu.make_async_copy(fv, gf_hbm, osem.at[3 + parts])
+    copy.start()
+    stores.append(copy)
+    for copy in stores:
+        copy.wait()
 
 
 def fused_shards(n, m, x_slab, filter_taps, mix_weight, skip_gain, cotangent):
@@ -403,20 +468,23 @@
     scale = 1.0 / math.sqrt(n * width)
     dma = pltpu.SemaphoreType.DMA
     vmem = pl.BlockSpec(memory_space=pltpu.VMEM)
-    anywhere = pl.BlockSpec(memory_space=pl.ANY)
-    gx, gw, gf = pl.pallas_call(
+    hbm = pl.BlockSpec(memory_space=pltpu.HBM)
+    weights = jnp.transpose(mix_weight, (1, 0, 2))
+    grads, x_rows, taps = pl.pallas_call(
         functools.partial(fused, n, m, scale),
         out_shape=(
-            jax.ShapeDtypeStruct((depth, width), bf16),
-            jax.ShapeDtypeStruct((3, rows, total), f32),
+            jax.ShapeDtypeStruct((3 * total, n * width), bf16),
+            jax.ShapeDtypeStruct((rows, n * width), bf16),
             jax.ShapeDtypeStruct((chans, width), f32),
         ),
-        in_specs=[anywhere, vmem, anywhere, pl.BlockSpec(memory_space=pltpu.SMEM), vmem],
-        out_specs=(vmem, vmem, vmem),
+        in_specs=[hbm] * 5,
+        out_specs=(vmem, hbm, vmem),
         scratch_shapes=[
+            pltpu.VMEM((chans, width), f32),
+            pltpu.VMEM((chans, width), bf16),
+            pltpu.SMEM((chans,), f32),
             pltpu.VMEM((depth, width), bf16),
             pltpu.VMEM((depth, 3 * total), bf16),
-            pltpu.VMEM((rows, n * width), bf16),
             pltpu.VMEM((chans, width), f32),
             pltpu.VMEM((n, 2 * PER_OWNER, width), f32),
             pltpu.VMEM((n, 2 * PER_OWNER, width), f32),
@@ -430,11 +498,10 @@
             pltpu.VMEM((PER_OWNER, n * width, width), bf16),
             pltpu.VMEM((m * n, 3 * chans, width), bf16),
             pltpu.VMEM((m * n * 3 * chans, width), f32),
-            pltpu.VMEM((3 * total, n * width), bf16),
             pltpu.VMEM((n, PER_OWNER, width), f32),
             pltpu.VMEM((n, PER_OWNER, width), f32),
-            dma((5,)),
-            dma((n,)), dma((n,)),
+            dma((8,)),
+            dma((3 * n,)), dma((3 * n,)),
             dma((n,)), dma((n,)),
             dma((m,)), dma((m,)),
             dma((n,)), dma((n,)),
@@ -442,9 +509,30 @@
             dma((n + 1 + 2 * (n - 1) + n,)), dma((m * n,)),
         ],
         compiler_params=pltpu.CompilerParams(
-            collective_id=0, has_side_effects=True, vmem_limit_bytes=40 * 1024 * 1024
+            collective_id=0, has_side_effects=True, vmem_limit_bytes=60 * 1024 * 1024
         ),
-    )(x_slab, filter_taps, jnp.transpose(mix_weight, (1, 0, 2)), skip_gain, cotangent)
+    )(x_slab, filter_taps, weights, skip_gain, cotangent)
+    parts = 4
+    gx, gw, gf = pl.pallas_call(
+        functools.partial(finish, parts, scale),
+        out_shape=(
+            jax.ShapeDtypeStruct((depth, width), bf16),
+            jax.ShapeDtypeStruct((3, rows, total), f32),
+            jax.ShapeDtypeStruct((chans, width), f32),
+        ),
+        in_specs=[hbm] * 4,
+        out_specs=(hbm, hbm, hbm),
+        scratch_shapes=[
+            pltpu.VMEM((3 * total, n * width), bf16),
+            pltpu.VMEM((rows, n * width), bf16),
+            pltpu.VMEM((depth, 3 * total), bf16),
+            pltpu.VMEM((chans, width), f32),
+            pltpu.VMEM((depth, width), bf16),
+            pltpu.VMEM((3, rows, total), f32),
+            dma((3,)), dma((3 * parts,)), dma((4 + parts,)),
+        ],
+        compiler_params=pltpu.CompilerParams(vmem_limit_bytes=60 * 1024 * 1024),
+    )(grads, x_rows, weights, taps)
     return (gx, jnp.transpose(gw, (1, 0, 2)), gf)
 
 

time: 43.3 us -> 35.8 us (0.83)
  local copies, waits for them, and re-layouts: 6.66 us -> 0 us
  Pallas kernels: 35.7 us -> 35 us
    unnamed x13 -> x0, local copies, waits for them, and re-layouts: 6.66 us -> none
    pallas_call x1, Pallas kernels: 35.7 us -> 30.3 us  [fused_shards(): pl.pallas_call(functools.partial(fused, n, m, scale), out_shape=(jax.Shap...]
    pallas_call x0 -> x1, Pallas kernels: none -> 4.61 us  [fused_shards(): pl.pallas_call(functools.partial(finish, parts, scale), out_shape=(jax.Sh...]
where the time goes in v2:
time: 35.8 us; the launch traced here: 35.6 us
  Pallas kernels  35 us (98%)
  between operations  0.64 us (2%)
    pallas_call x1, Pallas kernels, fused_shards(): pl.pallas_call(functools.partial(fused, n, m, scale), out_shape=(jax.Shap...  30.3 us
    pallas_call x1, Pallas kernels, fused_shards(): pl.pallas_call(functools.partial(finish, parts, scale), out_shape=(jax.Sh...  4.61 us

profile of v2, /device:TPU:1, one launch (start us, length us, event | category | flops | bytes accessed | tf_op | source)
XLA Modules:
  0.0 35.6 jit_solution(9326397098045415553)
XLA Ops:
  0.6 30.3 %shard_map.76 = (bf16[384,1024]{1,0:T(8,128)(2,1)}, bf16[256,1024]{1,0:T(8,128)(2,1)}, f32[32,128]{1,0:T(8,128)}) custom-call(bf16[2048,128]{1,0:T(8,128)(2,1)} %x_hbm.1, f32[32,128]{1,0:T(8,128)} %f_hbm.1, bf16[3,2048,128]{2,1,0:T(8,128)(2,1)} %bitcast.2, f32[32]{0:T(128)} %gain_hbm.1, bf16[32,128]{1,0:T(8,128)(2,1)} %cot_hbm.1), custom_call_target="tpu_custom_call" | custom-call | tf_op jit(solution)/shard_map/pallas_call | solution.py:473
  31.0 4.6 %shard_map.77 = (bf16[2048,128]{1,0:T(8,128)(2,1)}, f32[3,256,128]{2,1,0:T(8,128)}, f32[32,128]{1,0:T(8,128)}) custom-call(bf16[384,1024]{1,0:T(8,128)(2,1)} %get-tuple-element.9.g_hbm, bf16[256,1024]{1,0:T(8,128)(2,1)} %get-tuple-element.10.x_hbm, bf16[3,2048,128]{2,1,0:T(8,128)(2,1)} %bitcast.3, f32[32,128]{1,0:T(8,128)} %get-tuple-element.11.f_hbm), custom_call_target="tpu_custom_call" | custom-call | tf_op jit(solution)/shard_map/pallas_call | solution.py:516

commit v3 on v2

--- a/solution.py
+++ b/solution.py
@@ -147,7 +147,7 @@
 
 MESH = pl.DeviceIdType.MESH
 PER_OWNER = 4
-CUTS = (0, 6, 10, 16)
+CUTS = (0, 5, 9, 16)
 
 
 def toeplitz(row, put):
@@ -181,10 +181,10 @@
 def fused(
     n, m, scale,
     x_hbm, f_hbm, w_hbm, gain_hbm, cot_hbm,
-    gmat, xall, gf_ref,
+    g_hbm, xall, gf_ref,
     f_ref, cot_ref, gain_ref, xv, wv, cot32, fsend, fall, part, psend, precv, csum, csend, call,
-    tcat, tvert, gall, gf32, fgs, fgall,
-    lsem, xs, xr, fs, fr, ps, pr, cs, cr, hs, hr, gs, gr,
+    tcat, tvert, gall, gf32, gmat, fgs, fgall,
+    osem, lsem, xs, xr, fs, fr, ps, pr, cs, cr, hs, hr, gs, gr,
 ):
     k = lax.axis_index("ctx")
     h = lax.axis_index("ch")
@@ -257,15 +257,6 @@
         fsend[q, 0:4, :] = f_ref[pl.ds(q, PER_OWNER, stride=n), :]
         fsend[q, 4:8, :] = cot32[pl.ds(q, PER_OWNER, stride=n), :]
     fall[k] = fsend[k]
-    pl.semaphore_wait(barrier, n + m - 2)
-
-    for i in range(1, n):
-        kk = lax.rem(k + i, n)
-        copy = remote(fsend.at[kk], fall.at[k], fs.at[i], fr.at[k], kk, h)
-        copy.start()
-        sends.append(copy)
-    send_x(0)
-
     load_x.wait()
     for copy in load_w:
         copy.wait()
@@ -276,11 +267,19 @@
             cut = piece[q * chans : (q + 1) * chans]
             part[q, j * chans : (j + 1) * chans, :] = cut
             psend[q, j * chans : (j + 1) * chans, :] = cut.astype(bf16)
+    pl.semaphore_wait(barrier, n + m - 2)
     for i in range(1, m):
         hh = lax.rem(h + i, m)
         copy = remote(psend.at[hh], precv.at[h], ps.at[i], pr.at[h], k, hh)
         copy.start()
         sends.append(copy)
+    for i in range(1, n):
+        kk = lax.rem(k + i, n)
+        copy = remote(fsend.at[kk], fall.at[k], fs.at[i], fr.at[k], kk, h)
+        copy.start()
+        sends.append(copy)
+    send_x(0)
+
 
     for i in range(1, n):
         kk = lax.rem(k + n - i, n)
@@ -340,6 +339,31 @@
                 [made[c][j], made[c + 1][j]], axis=0
             ).astype(bf16)
 
+    block = 3 * chans
+    stores = []
+
+    def expand(place, hh):
+        base = place * n * block
+        for q in range(n):
+            gf32[base + q * block : base + (q + 1) * block, :] = gall[hh * n + q].astype(f32)
+        for j in range(3):
+            for c in range(0, PER_OWNER, 2):
+                start = pl.multiple_of(j * m * chans + hh * chans + c * n, 2 * n)
+                for b in range(n):
+                    pair = [
+                        gf32[pl.ds(base + j * chans + cc * n + b, n, stride=block), :]
+                        for cc in (c, c + 1)
+                    ]
+                    gmat[pl.ds(start, 2 * n), b * 128 : (b + 1) * 128] = jnp.concatenate(
+                        pair, axis=0
+                    ).astype(bf16)
+            span = pl.ds(pl.multiple_of(j * m * chans + hh * chans, chans), chans)
+            copy = pltpu.make_async_copy(
+                gmat.at[span, :], g_hbm.at[span, :], osem.at[place * 3 + j]
+            )
+            copy.start()
+            stores.append(copy)
+
     count = 0
 
     def push(slot, kk, hh, index):
@@ -369,11 +393,13 @@
         push(slot, k, y_h, count)
         push(slot, k, core_h, count + 1)
         count += 2
+    expand(0, h)
     for i in range(n):
         slot = y_h * n + lax.rem(k + n - i, n)
         landed(slot)
         push(slot, k, core_h, count)
         count += 1
+    expand(1, y_h)
     for i in range(1, n):
         kk = lax.rem(k + n - i, n)
         remote(fgs.at[kk], fgall.at[kk], hs.at[i], hr.at[kk], kk, h).wait_recv()
@@ -388,21 +414,10 @@
         for hh in (core_h, diag_h):
             landed(hh * n + lax.rem(k + n - i, n))
 
-    block = 3 * chans
-    for q in range(m * n):
-        gf32[q * block : (q + 1) * block, :] = gall[q].astype(f32)
-    for hh in range(m):
-        for j in range(3):
-            for c in range(0, PER_OWNER, 2):
-                for b in range(n):
-                    pair = [
-                        gf32[pl.ds(hh * n * block + j * chans + cc * n + b, n, stride=block), :]
-                        for cc in (c, c + 1)
-                    ]
-                    start = j * 128 + hh * chans + c * n
-                    gmat[start : start + 2 * n, b * 128 : (b + 1) * 128] = jnp.concatenate(
-                        pair, axis=0
-                    ).astype(bf16)
+    expand(2, core_h)
+    expand(3, diag_h)
+    for copy in stores:
+        copy.wait()
     for copy in sends:
         copy.wait_send()
 
@@ -478,7 +493,7 @@
             jax.ShapeDtypeStruct((chans, width), f32),
         ),
         in_specs=[hbm] * 5,
-        out_specs=(vmem, hbm, vmem),
+        out_specs=(hbm, hbm, vmem),
         scratch_shapes=[
             pltpu.VMEM((chans, width), f32),
             pltpu.VMEM((chans, width), bf16),
@@ -498,8 +513,10 @@
             pltpu.VMEM((PER_OWNER, n * width, width), bf16),
             pltpu.VMEM((m * n, 3 * chans, width), bf16),
             pltpu.VMEM((m * n * 3 * chans, width), f32),
+            pltpu.VMEM((3 * total, n * width), bf16),
             pltpu.VMEM((n, PER_OWNER, width), f32),
             pltpu.VMEM((n, PER_OWNER, width), f32),
+            dma((3 * m,)),
             dma((8,)),
             dma((3 * n,)), dma((3 * n,)),
             dma((n,)), dma((n,)),

time: 35.8 us -> 35.3 us (0.986)
  the two profiles are of different devices: /device:TPU:1 before, /device:TPU:25 now
where the time goes in v3:
time: 35.3 us; the launch traced here: 35.1 us
  Pallas kernels  34.4 us (97%)
  between operations  0.64 us (2%)
    pallas_call x1, Pallas kernels, fused_shards(): pl.pallas_call(functools.partial(fused, n, m, scale), out_shape=(jax.Shap...  29.8 us
    pallas_call x1, Pallas kernels, fused_shards(): pl.pallas_call(functools.partial(finish, parts, scale), out_shape=(jax.Sh...  4.61 us

profile of v3, /device:TPU:25, one launch (start us, length us, event | category | flops | bytes accessed | tf_op | source)
XLA Modules:
  0.0 35.1 jit_solution(1198772572730065200)
XLA Ops:
  0.6 29.8 %shard_map.76 = (bf16[384,1024]{1,0:T(8,128)(2,1)}, bf16[256,1024]{1,0:T(8,128)(2,1)}, f32[32,128]{1,0:T(8,128)}) custom-call(bf16[2048,128]{1,0:T(8,128)(2,1)} %x_hbm.1, f32[32,128]{1,0:T(8,128)} %f_hbm.1, bf16[3,2048,128]{2,1,0:T(8,128)(2,1)} %bitcast.2, f32[32]{0:T(128)} %gain_hbm.1, bf16[32,128]{1,0:T(8,128)(2,1)} %cot_hbm.1), custom_call_target="tpu_custom_call" | custom-call | tf_op jit(solution)/shard_map/pallas_call | solution.py:488
  30.5 4.6 %shard_map.77 = (bf16[2048,128]{1,0:T(8,128)(2,1)}, f32[3,256,128]{2,1,0:T(8,128)}, f32[32,128]{1,0:T(8,128)}) custom-call(bf16[384,1024]{1,0:T(8,128)(2,1)} %get-tuple-element.9.g_hbm, bf16[256,1024]{1,0:T(8,128)(2,1)} %get-tuple-element.10.x_hbm, bf16[3,2048,128]{2,1,0:T(8,128)(2,1)} %bitcast.3, f32[32,128]{1,0:T(8,128)} %get-tuple-element.11.f_hbm), custom_call_target="tpu_custom_call" | custom-call | tf_op jit(solution)/shard_map/pallas_call | solution.py:533

commit v4 on v3

--- a/solution.py
+++ b/solution.py
@@ -529,7 +529,7 @@
             collective_id=0, has_side_effects=True, vmem_limit_bytes=60 * 1024 * 1024
         ),
     )(x_slab, filter_taps, weights, skip_gain, cotangent)
-    parts = 4
+    parts = 2
     gx, gw, gf = pl.pallas_call(
         functools.partial(finish, parts, scale),
         out_shape=(

time: 35.3 us -> 34.7 us (0.983)
  Pallas kernels: 34.4 us -> 33.9 us
    pallas_call x1, Pallas kernels: 4.61 us -> 4.03 us  [fused_shards(): pl.pallas_call(functools.partial(finish, parts, scale), out_shape=(jax.Sh...]
where the time goes in v4:
time: 34.7 us; the launch traced here: 34.5 us
  Pallas kernels  33.9 us (98%)
  between operations  0.64 us (2%)
    pallas_call x1, Pallas kernels, fused_shards(): pl.pallas_call(functools.partial(fused, n, m, scale), out_shape=(jax.Shap...  29.8 us
    pallas_call x1, Pallas kernels, fused_shards(): pl.pallas_call(functools.partial(finish, parts, scale), out_shape=(jax.Sh...  4.03 us

profile of v4, /device:TPU:25, one launch (start us, length us, event | category | flops | bytes accessed | tf_op | source)
XLA Modules:
  0.0 34.5 jit_solution(2153775506271546393)
XLA Ops:
  0.6 29.8 %shard_map.76 = (bf16[384,1024]{1,0:T(8,128)(2,1)}, bf16[256,1024]{1,0:T(8,128)(2,1)}, f32[32,128]{1,0:T(8,128)}) custom-call(bf16[2048,128]{1,0:T(8,128)(2,1)} %x_hbm.1, f32[32,128]{1,0:T(8,128)} %f_hbm.1, bf16[3,2048,128]{2,1,0:T(8,128)(2,1)} %bitcast.2, f32[32]{0:T(128)} %gain_hbm.1, bf16[32,128]{1,0:T(8,128)(2,1)} %cot_hbm.1), custom_call_target="tpu_custom_call" | custom-call | tf_op jit(solution)/shard_map/pallas_call | solution.py:488
  30.5 4.0 %shard_map.77 = (bf16[2048,128]{1,0:T(8,128)(2,1)}, f32[3,256,128]{2,1,0:T(8,128)}, f32[32,128]{1,0:T(8,128)}) custom-call(bf16[384,1024]{1,0:T(8,128)(2,1)} %get-tuple-element.9.g_hbm, bf16[256,1024]{1,0:T(8,128)(2,1)} %get-tuple-element.10.x_hbm, bf16[3,2048,128]{2,1,0:T(8,128)(2,1)} %bitcast.3, f32[32,128]{1,0:T(8,128)} %get-tuple-element.11.f_hbm), custom_call_target="tpu_custom_call" | custom-call | tf_op jit(solution)/shard_map/pallas_call | solution.py:533
